TPU v7x, 32 devices: a whole 2x2x4 slice. The times are simulated.
32 devices in a mesh: region: 4 (over y, core), var: 8 (over z, x).
Axes of the slice: x: 2, y: 2, z: 4, core: 2. Of those that a mesh axis runs over, the one named last changes fastest.
Arguments:
- state: float32 [16384, 768], P(('region', 'var')), may hold values from -6 to 6
- taper: bfloat16 [4, 16384, 384], P(None, ('region', 'var')), may hold values from 0.19921875 to 1
- block_mask: int32 [4, 128, 3], P(None, ('region', 'var')), may hold values 0 or 1
- anom_fly: float32 [4, 384, 768], P('region', 'var'), may hold values from -6 to 6
- incr_fly: float32 [4, 384, 768], P('region', 'var'), may hold values from -6 to 6
- anom_new: float32 [3, 384, 768], P(None, 'var'), may hold values from -6 to 6
- incr_new: float32 [3, 384, 768], P(None, 'var'), may hold values from -6 to 6
Outputs:
- updated: float32 [16384, 768], P(('region', 'var'))
All inputs are finite; a program needn't handle non-finite values. No bound on the sum of `block_mask` on one device may be relied on, other than what follows from the above.
Results may differ from a plain program's by a relative error of at most 0.0003.
Values sent between devices are 32-bit elements; how exact they have to be, the bound alone decides.
A program may use at most 64 MiB of HBM per device.

v0:
```python
import jax
import jax.numpy as jnp
from jax import lax
from jax.sharding import PartitionSpec as P

MEMBERS = 768
BLOCK = 128
TICKS = 4


def shifted(block, axis, distance):
    devices = range(lax.axis_size(axis))
    route = [(i - distance, i) for i in devices if i - distance in devices]
    return lax.ppermute(block, axis, route)


def localizer(taper_now, block_flags):
    row_blocks, obs_blocks = block_flags.shape
    expanded = jnp.broadcast_to(
        block_flags[:, None, :, None], (row_blocks, BLOCK, obs_blocks, BLOCK)
    )
    expanded = expanded.reshape(row_blocks * BLOCK, obs_blocks * BLOCK).astype(jnp.float32)
    return taper_now.astype(jnp.float32) * expanded


def assimilate(state_rows, taper_now, block_flags, batch_pair):
    localize = localizer(taper_now, block_flags)
    gathered = lax.all_gather(batch_pair, "var", axis=1, tiled=True)
    covar = lax.dot_general(
        state_rows,
        gathered[0],
        (((1,), (1,)), ((), ())),
        precision=lax.Precision.HIGHEST,
        preferred_element_type=jnp.float32,
    )
    weights = localize * covar / (MEMBERS - 1)
    increment = jnp.dot(
        weights, gathered[1], precision=lax.Precision.HIGHEST, preferred_element_type=jnp.float32
    )
    return state_rows + increment


def on_device(state, taper, block_mask, anom_fly, incr_fly, anom_new, incr_new):
    region_id = lax.axis_index("region")
    in_flight = jnp.stack([anom_fly[0], incr_fly[0]])
    entering = jnp.stack([anom_new, incr_new], 1)
    state_rows = state
    batch_pair = in_flight
    for tick_num in range(TICKS):
        if tick_num > 0:
            distant = shifted(in_flight, "region", tick_num)
            enter_slot = jnp.clip(tick_num - 1 - region_id, 0, TICKS - 2)
            newcomer = lax.dynamic_index_in_dim(entering, enter_slot, 0, keepdims=False)
            batch_pair = jnp.where(region_id < tick_num, newcomer, distant)
        state_rows = assimilate(state_rows, taper[tick_num], block_mask[tick_num], batch_pair)
    return state_rows


def solution(mesh):
    in_specs = (
        P(("region", "var"), None),
        P(None, ("region", "var"), None),
        P(None, ("region", "var"), None),
        P("region", "var", None),
        P("region", "var", None),
        P(None, "var", None),
        P(None, "var", None),
    )
    out_specs = P(("region", "var"), None)
    return jax.shard_map(
        on_device, mesh=mesh, in_specs=in_specs, out_specs=out_specs, check_vma=False
    )
```

profile of v0, /device:TPU:0, one launch (start us, length us, event | category | flops | bytes accessed | tf_op | source)
XLA Modules:
  0.0 236.4 jit_solution(1025055115002796828)
XLA Ops:
  6.5 0.9 constant_dynamic-update-slice_fusion.1
  7.5 0.9 constant_dynamic-update-slice_fusion
  8.4 0.7 copy-done.6
  9.2 4.3 %collective-permute-start.2 = (f32[2,48,768]{2,1,0:T(8,128)}, f32[2,48,768]{2,1,0:T(8,128)S(1)}, u32[]{:S(2)}, u32[]{:S(2)}) collective-permute-start(f32[2,48,768]{2,1,0:T(8,128)} %copy-done.6), channel_id=1, source_target_pairs={{0,24},{1,25},{2,26},{3,27},{4,28},{5,29},{6,30},{7,31}} | collective-permute-start | bytes 884744 | tf_op jit(solution)/shard_map/ppermute | solution.py:14
  13.5 1.3 collective-permute-start
  14.8 2.3 collective-permute-start.1
  17.1 3.4 %collective-permute-done.2 = f32[2,48,768]{2,1,0:T(8,128)S(1)} collective-permute-done((f32[2,48,768]{2,1,0:T(8,128)}, f32[2,48,768]{2,1,0:T(8,128)S(1)}, u32[]{:S(2)}, u32[]{:S(2)}) %collective-permute-start.2) | collective-permute-done | bytes 294944 | tf_op jit(solution)/shard_map/ppermute | solution.py:14
  20.6 6.3 %collective-permute-done.1 = f32[2,48,768]{2,1,0:T(8,128)S(1)} collective-permute-done((f32[2,48,768]{2,1,0:T(8,128)}, f32[2,48,768]{2,1,0:T(8,128)S(1)}, u32[]{:S(2)}, u32[]{:S(2)}) %collective-permute-start.1) | collective-permute-done | bytes 294944 | tf_op jit(solution)/shard_map/ppermute | solution.py:14
  26.9 2.3 fusion.7
  29.3 0.7 all-gather.9.cloned.1.call-update
  30.0 0.5 all-gather.11.cloned.1.call-update
  30.6 0.6 fusion.15
  31.6 0.2 copy.42
  32.0 0.9 copy.44
  33.1 1.0 copy.46
  34.2 0.2 copy.48
  34.4 29.8 %all-gather.5.cloned.1.call-done = f32[2,384,768]{2,1,0:T(8,128)} async-done(((f32[2,48,768]{2,1,0:T(8,128)}), f32[2,384,768]{2,1,0:T(8,128)}) %all-gather.5.cloned.1.call-update) | async-done | bytes 2359312 | tf_op jit(solution)/shard_map/all_gather | solution.py:28
  64.2 0.2 broadcast_in_dim.8
  64.4 3.5 %fusion.1 = f32[512,384]{0,1:T(8,128)S(1)} fusion(f32[512,768]{1,0:T(8,128)S(1)} %copy-done, f32[2,384,768]{2,1,0:T(8,128)} %all-gather.5.cloned.1.call-done, f32[48,8,4,128]{3,2,1,0:T(4,128)S(1)} %bitcast.104, bf16[1,512,384]{1,2,0:T(8,128)(2,1)S(1)} %copy.42), kind=kOutput, calls=%fused_computation.9 | convolution fusion | flops 1812725760 | bytes 4718592 | tf_op jit(solution)/shard_map/dot_general | solution.py:29
  68.0 2.8 %convolution_add_fusion.3 = f32[512,768]{1,0:T(8,128)S(1)} fusion(f32[512,768]{1,0:T(8,128)S(1)} %copy-done, f32[512,384]{0,1:T(8,128)S(1)} %fusion.1, f32[2,384,768]{2,1,0:T(8,128)S(1)} %copy-done.1), kind=kOutput, calls=%fused_computation.3 | convolution fusion | flops 1812332544 | bytes 5111808 | tf_op jit(solution)/shard_map/dot_general | solution.py:37
  70.7 46.2 %all-gather.7.cloned.1.call-done = f32[2,384,768]{2,1,0:T(8,128)} async-done(((f32[2,48,768]{2,1,0:T(8,128)}), f32[2,384,768]{2,1,0:T(8,128)}) %all-gather.7.cloned.1.call-update) | async-done | bytes 2359312 | tf_op jit(solution)/shard_map/all_gather | solution.py:28
  116.9 0.2 broadcast_in_dim.9
  117.1 3.6 %fusion.2 = f32[512,384]{0,1:T(8,128)S(1)} fusion(f32[512,768]{1,0:T(8,128)S(1)} %convolution_add_fusion.3, f32[2,384,768]{2,1,0:T(8,128)} %all-gather.7.cloned.1.call-done, f32[48,8,4,128]{3,2,1,0:T(4,128)S(1)} %bitcast.105, bf16[1,512,384]{1,2,0:T(8,128)(2,1)} %copy.44), kind=kOutput, calls=%fused_computation.10 | convolution fusion | flops 1812725760 | bytes 4718592 | tf_op jit(solution)/shard_map/dot_general | solution.py:29
  120.7 2.8 %convolution_add_fusion.2 = f32[512,768]{1,0:T(8,128)S(1)} fusion(f32[512,768]{1,0:T(8,128)S(1)} %convolution_add_fusion.3, f32[512,384]{0,1:T(8,128)S(1)} %fusion.2, f32[2,384,768]{2,1,0:T(8,128)S(1)} %copy-done.4), kind=kOutput, calls=%fused_computation.2 | convolution fusion | flops 1812332544 | bytes 5111808 | tf_op jit(solution)/shard_map/dot_general | solution.py:37
  123.5 46.2 %all-gather.9.cloned.1.call-done = f32[2,384,768]{2,1,0:T(8,128)} async-done(((f32[2,48,768]{2,1,0:T(8,128)}), f32[2,384,768]{2,1,0:T(8,128)}) %all-gather.9.cloned.1.call-update) | async-done | bytes 2359312 | tf_op jit(solution)/shard_map/all_gather | solution.py:28
  169.7 0.2 broadcast_in_dim.10
  169.9 3.8 %fusion.3 = f32[512,384]{0,1:T(8,128)S(1)} fusion(f32[512,768]{1,0:T(8,128)S(1)} %convolution_add_fusion.2, f32[2,384,768]{2,1,0:T(8,128)} %all-gather.9.cloned.1.call-done, f32[48,8,4,128]{3,2,1,0:T(4,128)S(1)} %bitcast.106, bf16[1,512,384]{1,2,0:T(8,128)(2,1)} %copy.46), kind=kOutput, calls=%fused_computation.11 | convolution fusion | flops 1812725760 | bytes 4718592 | tf_op jit(solution)/shard_map/dot_general | solution.py:29
  173.8 2.8 %convolution_add_fusion.1 = f32[512,768]{1,0:T(8,128)S(1)} fusion(f32[512,768]{1,0:T(8,128)S(1)} %convolution_add_fusion.2, f32[512,384]{0,1:T(8,128)S(1)} %fusion.3, f32[2,384,768]{2,1,0:T(8,128)S(1)} %copy-done.3), kind=kOutput, calls=%fused_computation.1 | convolution fusion | flops 1812332544 | bytes 5111808 | tf_op jit(solution)/shard_map/dot_general | solution.py:37
  176.6 45.7 %all-gather.11.cloned.1.call-done = f32[2,384,768]{2,1,0:T(8,128)} async-done(((f32[2,48,768]{2,1,0:T(8,128)}), f32[2,384,768]{2,1,0:T(8,128)}) %all-gather.11.cloned.1.call-update) | async-done | bytes 2359312 | tf_op jit(solution)/shard_map/all_gather | solution.py:28
  222.3 0.2 broadcast_in_dim.11
  222.5 3.5 %fusion.4 = f32[512,384]{0,1:T(8,128)S(1)} fusion(f32[512,768]{1,0:T(8,128)S(1)} %convolution_add_fusion.1, f32[2,384,768]{2,1,0:T(8,128)} %all-gather.11.cloned.1.call-done, f32[48,8,4,128]{3,2,1,0:T(4,128)S(1)} %bitcast.107, bf16[1,512,384]{1,2,0:T(8,128)(2,1)S(1)} %copy.48), kind=kOutput, calls=%fused_computation.12 | convolution fusion | flops 1812725760 | bytes 4718592 | tf_op jit(solution)/shard_map/dot_general | solution.py:29
  226.0 3.9 %convolution_add_fusion = f32[512,768]{1,0:T(8,128)} fusion(f32[512,768]{1,0:T(8,128)S(1)} %convolution_add_fusion.1, f32[512,384]{0,1:T(8,128)S(1)} %fusion.4, f32[2,384,768]{2,1,0:T(8,128)S(1)} %copy-done.2), kind=kOutput, calls=%fused_computation | convolution fusion | flops 1812332544 | bytes 5111808 | tf_op jit(solution)/shard_map/dot_general | solution.py:37
  (39 shorter events, 1.1 us)
Async XLA Ops:
  6.5 57.7 %all-gather.5.cloned.1.call-start = ((), (), s32[]{:S(2)}) async-start(), calls=%async_computation | async-start | bytes 2654208 | tf_op jit(solution)/shard_map/all_gather | solution.py:28
  8.4 0.7 copy-start.6
  9.1 107.8 %all-gather.7.cloned.1.call-start = ((), (), s32[]{:S(2)}) async-start(), calls=%async_computation.1 | async-start | bytes 2654208 | tf_op jit(solution)/shard_map/all_gather | solution.py:28
  9.2 11.4 %collective-permute-start.2 = (f32[2,48,768]{2,1,0:T(8,128)}, f32[2,48,768]{2,1,0:T(8,128)S(1)}, u32[]{:S(2)}, u32[]{:S(2)}) collective-permute-start(f32[2,48,768]{2,1,0:T(8,128)} %copy-done.6), channel_id=1, source_target_pairs={{0,24},{1,25},{2,26},{3,27},{4,28},{5,29},{6,30},{7,31}} | collective-permute-start | bytes 884744 | tf_op jit(solution)/shard_map/ppermute | solution.py:14
  13.5 7.1 %collective-permute-start = (f32[2,48,768]{2,1,0:T(8,128)}, f32[2,48,768]{2,1,0:T(8,128)S(1)}, u32[]{:S(2)}, u32[]{:S(2)}) collective-permute-start(f32[2,48,768]{2,1,0:T(8,128)} %copy-done.6), channel_id=1, source_target_pairs={{0,8},{8,16},{16,24},{1,9},{9,17},{17,25},{2,10},{10,18},{18,26},{... | collective-permute-start | bytes 884744 | tf_op jit(solution)/shard_map/ppermute | solution.py:14
  14.8 12.1 %collective-permute-start.1 = (f32[2,48,768]{2,1,0:T(8,128)}, f32[2,48,768]{2,1,0:T(8,128)S(1)}, u32[]{:S(2)}, u32[]{:S(2)}) collective-permute-start(f32[2,48,768]{2,1,0:T(8,128)} %copy-done.6), channel_id=1, source_target_pairs={{0,16},{8,24},{1,17},{9,25},{2,18},{10,26},{3,19},{11,27},{4,20},{... | collective-permute-start | bytes 884744 | tf_op jit(solution)/shard_map/ppermute | solution.py:14
  26.9 3.7 %copy-start.9 = (s32[4,4,3]{1,0,2:T(4,128)S(1)}, s32[4,4,3]{1,0,2:T(4,128)}, u32[]{:S(2)}) copy-start(s32[4,4,3]{1,0,2:T(4,128)} %param.9) | copy-start | bytes 580
  26.9 4.5 %copy-start.5 = (bf16[4,512,384]{2,1,0:T(8,128)(2,1)S(1)}, bf16[4,512,384]{2,1,0:T(8,128)(2,1)}, u32[]{:S(2)}) copy-start(bf16[4,512,384]{2,1,0:T(8,128)(2,1)} %param.8) | copy-start | bytes 4718596
  29.3 140.5 %all-gather.9.cloned.1.call-start = ((), (), s32[]{:S(2)}) async-start(), calls=%async_computation.2 | async-start | bytes 2654208 | tf_op jit(solution)/shard_map/all_gather | solution.py:28
  30.0 192.3 %all-gather.11.cloned.1.call-start = ((), (), s32[]{:S(2)}) async-start(), calls=%async_computation.3 | async-start | bytes 2654208 | tf_op jit(solution)/shard_map/all_gather | solution.py:28
  31.5 1.4 copy-start.8
  31.5 2.5 %copy-start.7 = (s32[1,4,3]{1,0,2:T(1,128)S(1)}, s32[1,4,3]{1,0,2:T(1,128)}, u32[]{:S(2)}) copy-start(s32[1,4,3]{1,0,2:T(1,128)} %get-tuple-element.12) | copy-start | bytes 148
  31.9 32.4 %copy-start = (f32[512,768]{1,0:T(8,128)S(1)}, f32[512,768]{1,0:T(8,128)}, u32[]{:S(2)}) copy-start(f32[512,768]{1,0:T(8,128)} %param.7) | copy-start | bytes 4718596
  64.4 3.5 %copy-start.1 = (f32[2,384,768]{2,1,0:T(8,128)S(1)}, f32[2,384,768]{2,1,0:T(8,128)}, u32[]{:S(2)}) copy-start(f32[2,384,768]{2,1,0:T(8,128)} %all-gather.5.cloned.1.call-done) | copy-start | bytes 7077892
  117.1 3.6 %copy-start.4 = (f32[2,384,768]{2,1,0:T(8,128)S(1)}, f32[2,384,768]{2,1,0:T(8,128)}, u32[]{:S(2)}) copy-start(f32[2,384,768]{2,1,0:T(8,128)} %all-gather.7.cloned.1.call-done) | copy-start | bytes 7077892
  169.9 3.8 %copy-start.3 = (f32[2,384,768]{2,1,0:T(8,128)S(1)}, f32[2,384,768]{2,1,0:T(8,128)}, u32[]{:S(2)}) copy-start(f32[2,384,768]{2,1,0:T(8,128)} %all-gather.9.cloned.1.call-done) | copy-start | bytes 7077892
  222.5 3.5 %copy-start.2 = (f32[2,384,768]{2,1,0:T(8,128)S(1)}, f32[2,384,768]{2,1,0:T(8,128)}, u32[]{:S(2)}) copy-start(f32[2,384,768]{2,1,0:T(8,128)} %all-gather.11.cloned.1.call-done) | copy-start | bytes 7077892
Sparse Core Ops, SparseCore 0:
  9.5 54.6 all-gather.4
  66.4 50.4 all-gather.6
  119.1 50.6 all-gather.8
  171.8 50.4 all-gather.10
where the time goes:
time: 237 us; the launch traced here: 236 us
  waiting for transfers between devices  179 us (76%)
  matrix products  26.7 us (11%)
  between operations  13.4 us (6%)
  starting transfers between devices  8.05 us (3%)
  local copies, waits for them, and re-layouts  7.04 us (3%)
    all_gather x4, waiting for transfers between devices, assimilate(): gathered = lax.all_gather(batch_pair, 'var', axis=1, tiled=True)  168 us
    dot_general x4, matrix products, assimilate(): lax.dot_general(state_rows, gathered[0], (((1,), (1,)), ((), ())), precis...  14.5 us
    dot_general x4, matrix products, assimilate(): jnp.dot(weights, gathered[1], precision=lax.Precision.HIGHEST, preferred_...  12.3 us
    ppermute x3, waiting for transfers between devices, shifted(): return lax.ppermute(block, axis, route)  9.75 us
    ppermute x3, starting transfers between devices, shifted(): return lax.ppermute(block, axis, route)  7.92 us
  transfers between devices with their start and end apart: 7, of which 6 were waited for; matrix products, arithmetic and copies ran while one was open for 11% of the time, Pallas kernels for 0%

commit v1 on v0

v1 whole, which is shorter than its diff:
```python
import functools
import math

import jax
import jax.numpy as jnp
from jax import lax
from jax.experimental import pallas as pl
from jax.experimental.pallas import tpu as pltpu
from jax.sharding import PartitionSpec as P

MESH = pl.DeviceIdType.MESH
CORES = 2
PARTS = 2
ORDER = {
    (0, 0): (0, 1, 2, 3, 4),
    (0, 1): (3, 0, 4, 1, 2),
    (1, 0): (0, 1, 2, 3, 4),
    (1, 1): (2, 0, 3, 1, 4),
}
NT = (((1,), (1,)), ((), ()))
NN = (((1,), (0,)), ((), ()))


def split(value):
    high = value.astype(jnp.bfloat16)
    return high, (value - high.astype(jnp.float32)).astype(jnp.bfloat16)


def dot3(left, right_high, right_low, dims):
    high, low = split(left)
    rows = left.shape[0]
    both = lax.dot_general(
        jnp.concatenate([high, low], 0), right_high, dims, preferred_element_type=jnp.float32
    )
    cross = lax.dot_general(high, right_low, dims, preferred_element_type=jnp.float32)
    return both[:rows] + (both[rows:] + cross)


def kernel(
    n_region, n_var, n_x, ticks,
    mask_ref, state_ref, taper_ref, anom_fly, incr_fly, anom_new, incr_new,
    out_ref,
    buf, y_high, y_low, d_high, d_low, stage, recv, sent, seed_sent,
):
    slots = ticks + 1
    n_y, n_z = n_region // CORES, n_var // n_x
    region, var = lax.axis_index("region"), lax.axis_index("var")
    y, core = region // CORES, region % CORES
    z, x = var // n_x, var % n_x
    odd = y % 2
    fly, new = (anom_fly, incr_fly), (anom_new, incr_new)
    members = state_ref.shape[1]
    shard = buf.shape[3]
    block = state_ref.shape[0] // mask_ref.shape[1]

    def pick(table):
        return jnp.where(
            odd == 0,
            jnp.where(core == 0, table[0, 0], table[0, 1]),
            jnp.where(core == 0, table[1, 0], table[1, 1]),
        )

    def is_common(parity, slot):
        return jnp.where(parity == 0, slot <= ticks - 2, slot >= 2)

    def is_plane(parity, part, slot):
        return jnp.logical_or(jnp.logical_not(is_common(parity, slot)), parity == part)

    barrier = pltpu.get_barrier_semaphore()
    greeted = jnp.int32(0)
    reach = min(2, n_y - 1)
    others = [(z + 1 < n_z, region, var + n_x), (z > 0, region, var - n_x),
              (x + 1 < n_x, region, var + 1), (x > 0, region, var - 1)]
    for dy in range(-reach, reach + 1):
        for c in range(CORES):
            here = jnp.logical_and(y + dy >= 0, y + dy < n_y)
            target = (y + dy) * CORES + c
            others.append((jnp.logical_and(here, target != region), target, var))
    for there, r, v in others:
        @pl.when(there)
        def _(r=r, v=v):
            pl.semaphore_signal(barrier, inc=1, device_id=(r, v), device_id_type=MESH)
        greeted = greeted + there.astype(jnp.int32)
    pl.semaphore_wait(barrier, greeted)

    def seeds(begin):
        for dy in range(0, reach + 1):
            for part in range(PARTS):
                slot = 2 * dy + 1 - core
                target = (y + dy) * CORES + part
                go = jnp.logical_and(slot < slots, is_plane((y + dy) % 2, part, slot))
                go = jnp.logical_and(go, y + dy < n_y)
                go = jnp.logical_and(go, target != region)

                @pl.when(go)
                def _(part=part, slot=slot, target=target, dy=dy):
                    copy = pltpu.make_async_remote_copy(
                        src_ref=fly[part].at[0],
                        dst_ref=buf.at[slot, part, var],
                        send_sem=seed_sent.at[dy, part],
                        recv_sem=recv.at[slot, part, var],
                        device_id=(target, var),
                        device_id_type=MESH,
                    )
                    if begin:
                        copy.start()
                    else:
                        copy.wait_send()

    for slot in range(slots):
        batch = 2 * y + 1 - slot
        for part in range(PARTS):
            mine = jnp.logical_and(core == part, is_plane(odd, part, slot))

            @pl.when(jnp.logical_and(mine, batch == region))
            def _(slot=slot, part=part):
                pltpu.make_async_copy(
                    fly[part].at[0], buf.at[slot, part, var], recv.at[slot, part, var]
                ).start()

            if slot >= 2:
                @pl.when(jnp.logical_and(mine, batch < 0))
                def _(slot=slot, part=part, batch=batch):
                    pltpu.make_async_copy(
                        new[part].at[jnp.maximum(-batch - 1, 0)],
                        buf.at[slot, part, var],
                        recv.at[slot, part, var],
                    ).start()
    seeds(True)

    def wait_item(slot, part, source):
        here = buf.at[slot, part, source]
        pltpu.make_async_copy(here, here, recv.at[slot, part, source]).wait()

    def copies(unit, slot, z_from, x_from, act):
        source = z_from * n_x + x_from
        plane = is_plane(odd, core, slot)
        x_first = jnp.logical_and(odd != core, slot == jnp.where(odd == 0, slots - 1, 1))
        along_z = jnp.logical_and(plane, jnp.logical_or(x_first, x_from == x))
        along_x = jnp.logical_and(
            plane, jnp.logical_or(jnp.logical_not(x_first), z_from == z)
        )
        up = jnp.logical_and(z_from <= z, z + 1 < n_z)
        down = jnp.logical_and(z_from >= z, z > 0)
        right = jnp.logical_and(x_from <= x, x + 1 < n_x)
        left = jnp.logical_and(x_from >= x, x > 0)
        across = jnp.logical_and(plane, is_common(odd, slot))
        near = jnp.where(core == 0, slot < slots - 1, slot > 0)
        routes = [
            (jnp.logical_and(along_z, up), region, var + n_x, slot),
            (jnp.logical_and(along_z, down), region, var - n_x, slot),
            (jnp.logical_and(along_x, right), region, var + 1, slot),
            (jnp.logical_and(along_x, left), region, var - 1, slot),
            (across, region + CORES * (1 - 2 * odd), var, slot + 2 * (1 - 2 * odd)),
            (near, region + 1 - 2 * core, var, slot),
        ]
        for way, (go, r, v, slot_there) in enumerate(routes):
            @pl.when(go)
            def _(way=way, r=r, v=v, slot_there=slot_there):
                act(pltpu.make_async_remote_copy(
                    src_ref=buf.at[slot, core, source],
                    dst_ref=buf.at[slot_there, core, source],
                    send_sem=sent.at[unit, source, way],
                    recv_sem=recv.at[slot_there, core, source],
                    device_id=(r, v),
                    device_id_type=MESH,
                ))

    def begin(copy):
        copy.start()

    def end(copy):
        copy.wait_send()

    def handle(unit, slot, z_from, x_from):
        wait_item(slot, core, z_from * n_x + x_from)
        copies(unit, slot, z_from, x_from, begin)

    def own(unit, want_plane):
        slot = pick({key: order[unit] for key, order in ORDER.items()})
        plane = is_plane(odd, core, slot)

        @pl.when(plane if want_plane else jnp.logical_not(plane))
        def _():
            handle(unit, slot, z, x)

    def items(unit, first, last):
        slot = pick({key: order[unit] for key, order in ORDER.items()})

        def body(n, carry):
            k = n // n_x
            far = (k + 1) // 2
            z_from = z + jnp.where(k % 2 == 1, far, -far)
            x_from = (x + n % n_x) % n_x

            @pl.when(jnp.logical_and(z_from >= 0, z_from < n_z))
            def _():
                handle(unit, slot, z_from, x_from)
            return carry

        lax.fori_loop(first, last, body, 0)

    n_items = (2 * n_z - 1) * n_x
    n_chunks = mask_ref.shape[1]

    def prepare(tick):
        slot = tick + 1 - core

        def arrive(source, carry):
            wait_item(slot, 1 - core, source)
            return carry

        lax.fori_loop(0, n_var, arrive, 0)
        for part, high, low in ((0, y_high, y_low), (1, d_high, d_low)):
            if shard % 16 == 0:
                def cut(source, carry, part=part, high=high, low=low):
                    rows = pl.ds(pl.multiple_of(source * shard, 16), shard)
                    high[rows, :], low[rows, :] = split(buf[slot, part, source])
                    return carry

                lax.fori_loop(0, n_var, cut, 0)
            else:
                for source in range(n_var):
                    stage[pl.ds(source * shard, shard), :] = buf[slot, part, source]
                high[...], low[...] = split(stage[...])

    def chunk(tick, c):
        rows = pl.ds(pl.multiple_of(c * block, block), block)
        rows_in = out_ref[rows, :]
        covar = dot3(rows_in, y_high[...], y_low[...], NT)
        taper_now = taper_ref[tick, rows, :].astype(jnp.float32)
        n_obs_blocks = mask_ref.shape[2]
        width = covar.shape[1] // n_obs_blocks
        pieces = []
        for b in range(n_obs_blocks):
            flag = mask_ref[tick, c, b].astype(jnp.float32) * (1.0 / (members - 1))
            cols = slice(b * width, (b + 1) * width)
            pieces.append(taper_now[:, cols] * covar[:, cols] * flag)
        weights = jnp.concatenate(pieces, 1)
        out_ref[rows, :] = rows_in + dot3(weights, d_high[...], d_low[...], NN)

    def tick_now(tick):
        prepare(tick)

        def body(c, carry):
            chunk(tick, c)
            return carry

        lax.fori_loop(0, n_chunks, body, 0)

    out_ref[...] = state_ref[...]
    own(0, True)
    for unit in range(slots):
        if unit + 1 < slots:
            own(unit + 1, True)
        own(unit, False)
        if unit == slots - 1:
            prepare(0)

            def mixed(c, carry):
                chunk(0, c)
                return carry

            edges = [1 + (n_items - 1) * c // n_chunks for c in range(n_chunks + 1)]
            for c in range(n_chunks):
                items(unit, edges[c], edges[c + 1])
                lax.fori_loop(c, c + 1, mixed, 0)
        else:
            items(unit, 1, n_items)
    lax.fori_loop(1, ticks, lambda tick, carry: (tick_now(tick), carry)[1], 0)

    seeds(False)
    for unit in range(slots):
        slot = pick({key: order[unit] for key, order in ORDER.items()})

        def body(source, carry, unit=unit, slot=slot):
            copies(unit, slot, source // n_x, source % n_x, end)
            return carry

        lax.fori_loop(0, n_var, body, 0)


def on_device(n_region, n_var, state, taper, block_mask, anom_fly, incr_fly, anom_new, incr_new):
    ticks = taper.shape[0]
    shard, members = anom_fly.shape[1:]
    obs = shard * n_var
    n_x = 2 ** (int(math.log2(n_var)) // 2)
    slots = ticks + 1
    vmem = pl.BlockSpec(memory_space=pltpu.VMEM)
    anywhere = pl.BlockSpec(memory_space=pl.ANY)
    flops = 3 * 4 * ticks * state.shape[0] * obs * members
    return pl.pallas_call(
        functools.partial(kernel, n_region, n_var, n_x, ticks),
        out_shape=jax.ShapeDtypeStruct(state.shape, jnp.float32),
        in_specs=[pl.BlockSpec(memory_space=pltpu.SMEM), vmem, vmem] + [anywhere] * 4,
        out_specs=vmem,
        scratch_shapes=[
            pltpu.VMEM((slots, PARTS, n_var, shard, members), jnp.float32),
            pltpu.VMEM((obs, members), jnp.bfloat16),
            pltpu.VMEM((obs, members), jnp.bfloat16),
            pltpu.VMEM((obs, members), jnp.bfloat16),
            pltpu.VMEM((obs, members), jnp.bfloat16),
            pltpu.VMEM((8, 128) if shard % 16 == 0 else (obs, members), jnp.float32),
            pltpu.SemaphoreType.DMA((slots, PARTS, n_var)),
            pltpu.SemaphoreType.DMA((slots, n_var, 6)),
            pltpu.SemaphoreType.DMA((3, PARTS)),
        ],
        compiler_params=pltpu.CompilerParams(
            collective_id=0, has_side_effects=True, vmem_limit_bytes=48 * 1024 * 1024
        ),
        cost_estimate=pl.CostEstimate(
            flops=flops, bytes_accessed=4 * state.size * 4, transcendentals=0
        ),
        name="gather_and_assimilate",
    )(block_mask, state, taper, anom_fly, incr_fly, anom_new, incr_new)


def solution(mesh):
    n_region, n_var = mesh.shape["region"], mesh.shape["var"]
    in_specs = (
        P(("region", "var"), None),
        P(None, ("region", "var"), None),
        P(None, ("region", "var"), None),
        P("region", "var", None),
        P("region", "var", None),
        P(None, "var", None),
        P(None, "var", None),
    )
    out_specs = P(("region", "var"), None)
    return jax.shard_map(
        functools.partial(on_device, n_region, n_var),
        mesh=mesh, in_specs=in_specs, out_specs=out_specs, check_vma=False,
    )
```

time: 237 us -> 115 us (0.49)
  waiting for transfers between devices: 179 us -> 0 us
  Pallas kernels: 0 us -> 106 us
  matrix products: 26.7 us -> 0 us
  between operations: 13.4 us -> 0.02 us
  starting transfers between devices: 8.05 us -> 0 us
    all_gather x4 -> x0, waiting for transfers between devices: 168 us -> none  [assimilate(): gathered = lax.all_gather(batch_pair, 'var', axis=1, tiled=True)]
    pallas_call x0 -> x1, Pallas kernels: none -> 106 us  [on_device(): pl.pallas_call(functools.partial(kernel, n_region, n_var, n_x, ticks), ou...]
    dot_general x8 -> x0, matrix products: 26.7 us -> none  [the longest x4 14.5 us: assimilate(): lax.dot_general(state_rows, gathered[0], (((1,), (1,)), ((), ())), precis...]
    ppermute x3 -> x0, waiting for transfers between devices: 9.75 us -> none  [shifted(): return lax.ppermute(block, axis, route)]
    ppermute x3 -> x0, starting transfers between devices: 7.92 us -> none  [shifted(): return lax.ppermute(block, axis, route)]
    unnamed x29 -> x14, local copies, waits for them, and re-layouts: 4.3 us -> 8.6 us
  transfers between devices with their start and end apart: 7 -> 0, of which waited for: 6 -> 0; matrix products, arithmetic and copies ran while one was open for 11% -> 0% of each run, Pallas kernels for 0% -> 0%
where the time goes in v1:
time: 115 us
  Pallas kernels  106 us (92%)
  local copies, waits for them, and re-layouts  8.6 us (7%)
    pallas_call x1, Pallas kernels, on_device(): pl.pallas_call(functools.partial(kernel, n_region, n_var, n_x, ticks), ou...  106 us
    unnamed x14, local copies, waits for them, and re-layouts  8.6 us

profile of v1, /device:TPU:0, one launch (start us, length us, event | category | flops | bytes accessed | tf_op | source)
XLA Modules:
  0.0 115.0 jit_solution(4737470697656211081)
XLA Ops:
  0.0 0.8 copy.8.mask_ref
  0.8 0.0 copy-start
  0.8 1.4 %copy-done = f32[512,768]{1,0:T(8,128)S(1)} copy-done((f32[512,768]{1,0:T(8,128)S(1)}, f32[512,768]{1,0:T(8,128)}, u32[]{:S(2)}) %copy-start) | copy-done | bytes 1572888
  2.2 0.0 copy-start.1
  2.2 1.4 %copy-done.1 = bf16[4,512,384]{2,1,0:T(8,128)(2,1)S(1)} copy-done((bf16[4,512,384]{2,1,0:T(8,128)(2,1)S(1)}, bf16[4,512,384]{2,1,0:T(8,128)(2,1)}, u32[]{:S(2)}) %copy-start.1) | copy-done | bytes 1572888
  3.6 0.0 copy-start.2
  3.6 1.0 copy-done.2
  4.6 0.0 copy-start.3
  4.6 1.0 copy-done.3
  5.6 0.0 copy-start.4
  5.6 0.9 copy-done.4
  6.6 0.0 copy-start.5
  6.6 0.9 copy-done.5
  7.5 106.4 %gather_and_assimilate.1 = f32[512,768]{1,0:T(8,128)S(1)} custom-call(s32[4,4,3]{2,1,0:T(4,128)S(1)} %copy.8.mask_ref, f32[512,768]{1,0:T(8,128)S(1)} %copy-done, bf16[4,512,384]{2,1,0:T(8,128)(2,1)S(1)} %copy-done.1, f32[1,48,768]{2,1,0:T(8,128)S(1)} %copy-done.4, f32[1,48,768]{2,1,0:T(8,128)S(1)} %copy-done.5, f32[3,48,768]{2,1,0:T(8,128)S(1)} %copy-done.2, ...), custom_call_target="tpu_custom_call" | custom-call | flops 7247757312 | bytes 6291456 | tf_op jit(solution)/shard_map/gather_and_assimilate/pallas_call | solution.py:292
  113.8 1.1 copy.10
Async XLA Ops:
  0.8 1.4 %copy-start = (f32[512,768]{1,0:T(8,128)S(1)}, f32[512,768]{1,0:T(8,128)}, u32[]{:S(2)}) copy-start(f32[512,768]{1,0:T(8,128)} %state_ref.1) | copy-start | bytes 4718596
  2.2 1.4 %copy-start.1 = (bf16[4,512,384]{2,1,0:T(8,128)(2,1)S(1)}, bf16[4,512,384]{2,1,0:T(8,128)(2,1)}, u32[]{:S(2)}) copy-start(bf16[4,512,384]{2,1,0:T(8,128)(2,1)} %taper_ref.1) | copy-start | bytes 4718596
  3.6 1.0 copy-start.2
  4.6 1.0 copy-start.3
  5.6 0.9 copy-start.4
  6.6 0.9 copy-start.5

commit v2 on v1

v2 whole, which is shorter than its diff:
```python
import functools
import math

import jax
import jax.numpy as jnp
from jax import lax
from jax.experimental import pallas as pl
from jax.experimental.pallas import tpu as pltpu
from jax.sharding import PartitionSpec as P

MESH = pl.DeviceIdType.MESH
CORES = 2
PARTS = 2
UNITS = {
    (0, 0): ((0, 0), (1, 0), (2, 0), (3, 0)),
    (0, 1): ((3, 1), (4, 1), (4, 0)),
    (1, 0): ((0, 0), (0, 1), (1, 0), (1, 1)),
    (1, 1): ((2, 1), (3, 1), (4, 1)),
}
N_UNITS = 4
N_SHARED = 3
AHEAD = 2
NT = (((1,), (1,)), ((), ()))
NN = (((1,), (0,)), ((), ()))


def split(value):
    high = value.astype(jnp.bfloat16)
    return high, (value - high.astype(jnp.float32)).astype(jnp.bfloat16)


def dot3(left, right_high, right_low, dims):
    high, low = split(left)
    rows = left.shape[0]
    both = lax.dot_general(
        jnp.concatenate([high, low], 0), right_high, dims, preferred_element_type=jnp.float32
    )
    cross = lax.dot_general(high, right_low, dims, preferred_element_type=jnp.float32)
    return both[:rows] + (both[rows:] + cross)


def kernel(
    n_region, n_var, n_x, ticks,
    mask_ref, state_ref, taper_hbm, anom_fly, incr_fly, anom_new, incr_new,
    out_ref,
    buf, taper_ref, y_high, y_low, d_high, d_low, stage, recv, sent, seed_sent, load,
):
    slots = ticks + 1
    n_y, n_z = n_region // CORES, n_var // n_x
    region, var = lax.axis_index("region"), lax.axis_index("var")
    y, core = region // CORES, region % CORES
    z, x = var // n_x, var % n_x
    odd = y % 2
    fly, new = (anom_fly, incr_fly), (anom_new, incr_new)
    members = state_ref.shape[1]
    shard = buf.shape[3]
    block = state_ref.shape[0] // mask_ref.shape[1]

    state_load = pltpu.make_async_copy(state_ref, out_ref, load.at[0])
    taper_load = pltpu.make_async_copy(taper_hbm, taper_ref, load.at[1])
    state_load.start()
    taper_load.start()

    def choose(parity, mate, table):
        return jnp.where(
            parity == 0,
            jnp.where(mate == 0, table[0, 0], table[0, 1]),
            jnp.where(mate == 0, table[1, 0], table[1, 1]),
        )

    def is_carried(parity, mate, slot, part):
        def listed(pairs):
            found = False
            for unit_slot, unit_part in pairs:
                if unit_part == part:
                    found = jnp.logical_or(found, slot == unit_slot)
            return jnp.asarray(found)
        return choose(parity, mate, {key: listed(pairs) for key, pairs in UNITS.items()})

    def is_shared(parity, slot):
        return jnp.where(parity == 0, slot < N_SHARED, slot >= slots - N_SHARED)

    def carrier(slot, part):
        here = jnp.logical_and(is_shared(odd, slot), odd != part)
        return jnp.where(
            is_carried(odd, 0, slot, part), 0, jnp.where(here, part, 1)
        )

    barrier = pltpu.get_barrier_semaphore()
    greeted = jnp.int32(0)
    reach = min(2, n_y - 1)
    others = [(z + 1 < n_z, region, var + n_x), (z > 0, region, var - n_x),
              (x + 1 < n_x, region, var + 1), (x > 0, region, var - 1)]
    for dy in range(-reach, reach + 1):
        for c in range(CORES):
            here = jnp.logical_and(y + dy >= 0, y + dy < n_y)
            target = (y + dy) * CORES + c
            others.append((jnp.logical_and(here, target != region), target, var))
    for there, r, v in others:
        @pl.when(there)
        def _(r=r, v=v):
            pl.semaphore_signal(barrier, inc=1, device_id=(r, v), device_id_type=MESH)
        greeted = greeted + there.astype(jnp.int32)
    pl.semaphore_wait(barrier, greeted)

    def seeds(begin):
        for dy in range(0, reach + 1):
            for mate in range(CORES):
                slot = 2 * dy + 1 - core
                target = (y + dy) * CORES + mate
                for part in range(PARTS):
                    go = jnp.logical_and(
                        slot < slots, is_carried((y + dy) % 2, mate, slot, part)
                    )
                    go = jnp.logical_and(go, y + dy < n_y)
                    go = jnp.logical_and(go, target != region)

                    @pl.when(go)
                    def _(part=part, slot=slot, target=target, dy=dy, mate=mate):
                        copy = pltpu.make_async_remote_copy(
                            src_ref=fly[part].at[0],
                            dst_ref=buf.at[slot, part, var],
                            send_sem=seed_sent.at[dy, mate, part],
                            recv_sem=recv.at[slot, part, var],
                            device_id=(target, var),
                            device_id_type=MESH,
                        )
                        if begin:
                            copy.start()
                        else:
                            copy.wait_send()

    for slot in range(slots):
        batch = 2 * y + 1 - slot
        for part in range(PARTS):
            mine = is_carried(odd, core, slot, part)

            @pl.when(jnp.logical_and(mine, batch == region))
            def _(slot=slot, part=part):
                pltpu.make_async_copy(
                    fly[part].at[0], buf.at[slot, part, var], recv.at[slot, part, var]
                ).start()

            if slot >= 2:
                @pl.when(jnp.logical_and(mine, batch < 0))
                def _(slot=slot, part=part, batch=batch):
                    pltpu.make_async_copy(
                        new[part].at[jnp.maximum(-batch - 1, 0)],
                        buf.at[slot, part, var],
                        recv.at[slot, part, var],
                    ).start()
    seeds(True)

    def wait_item(slot, part, source):
        here = buf.at[slot, part, source]
        pltpu.make_async_copy(here, here, recv.at[slot, part, source]).wait()

    def plane_unit(unit):
        pairs = {key: units[min(unit, len(units) - 1)] for key, units in UNITS.items()}
        slot = choose(odd, core, {key: pair[0] for key, pair in pairs.items()})
        part = choose(odd, core, {key: pair[1] for key, pair in pairs.items()})
        there = choose(odd, core, {key: unit < len(units) for key, units in UNITS.items()})
        return slot, part, there

    def shared_unit(unit):
        return unit + (slots - N_SHARED) * odd, 1 - odd, core != odd

    def near_copy(slot, part, source, send_sem, act):
        @pl.when(jnp.where(core == 0, slot < slots - 1, slot > 0))
        def _():
            act(pltpu.make_async_remote_copy(
                src_ref=buf.at[slot, part, source],
                dst_ref=buf.at[slot, part, source],
                send_sem=send_sem,
                recv_sem=recv.at[slot, part, source],
                device_id=(region + 1 - 2 * core, var),
                device_id_type=MESH,
            ))

    def copies(unit, slot, part, z_from, x_from, act):
        source = z_from * n_x + x_from
        x_first = jnp.where(
            odd == 0,
            jnp.logical_and(slot == slots - 1, part == 1),
            jnp.logical_and(slot == 1, part == 0),
        )
        along_z = jnp.logical_or(x_first, x_from == x)
        along_x = jnp.logical_or(jnp.logical_not(x_first), z_from == z)
        up = jnp.logical_and(z_from <= z, z + 1 < n_z)
        down = jnp.logical_and(z_from >= z, z > 0)
        right = jnp.logical_and(x_from <= x, x + 1 < n_x)
        left = jnp.logical_and(x_from >= x, x > 0)
        across = is_shared(odd, slot)
        routes = [
            (jnp.logical_and(along_z, up), region, var + n_x, slot),
            (jnp.logical_and(along_z, down), region, var - n_x, slot),
            (jnp.logical_and(along_x, right), region, var + 1, slot),
            (jnp.logical_and(along_x, left), region, var - 1, slot),
            (across, region + CORES * (1 - 2 * odd), var, slot + 2 * (1 - 2 * odd)),
        ]
        for way, (go, r, v, slot_there) in enumerate(routes):
            @pl.when(go)
            def _(way=way, r=r, v=v, slot_there=slot_there):
                act(pltpu.make_async_remote_copy(
                    src_ref=buf.at[slot, part, source],
                    dst_ref=buf.at[slot_there, part, source],
                    send_sem=sent.at[unit, source, way],
                    recv_sem=recv.at[slot_there, part, source],
                    device_id=(r, v),
                    device_id_type=MESH,
                ))
        near_copy(slot, part, source, sent.at[unit, source, len(routes)], act)

    def begin(copy):
        copy.start()

    def end(copy):
        copy.wait_send()

    def ring(hop, act):
        pairs = [
            (dz, dx)
            for ax in range(min(hop, n_x - 1) + 1)
            for dz in sorted({hop - ax, ax - hop}, reverse=True)
            for dx in sorted({ax, -ax}, reverse=True)
            if hop - ax < n_z
        ]
        for dz, dx in pairs:
            z_from, x_from = z + dz, x + dx
            inside = jnp.logical_and(z_from >= 0, z_from < n_z)
            inside = jnp.logical_and(inside, jnp.logical_and(x_from >= 0, x_from < n_x))

            @pl.when(inside)
            def _(z_from=z_from, x_from=x_from):
                act(z_from, x_from)

    def gather_step(unit, hop):
        slot, part, there = plane_unit(unit)

        def handle(z_from, x_from):
            wait_item(slot, part, z_from * n_x + x_from)
            copies(unit, slot, part, z_from, x_from, begin)

        @pl.when(there)
        def _():
            ring(hop, handle)

    def shared_step(unit, hop):
        slot, part, there = shared_unit(unit)

        def handle(z_from, x_from):
            source = z_from * n_x + x_from
            wait_item(slot, part, source)
            near_copy(slot, part, source, sent.at[N_UNITS + unit, source, 0], begin)

        @pl.when(there)
        def _():
            ring(hop, handle)

    per_chunk = 2 if mask_ref.shape[1] % 2 == 0 else 1
    n_chunks = mask_ref.shape[1] // per_chunk
    height = per_chunk * block

    def prepare(tick):
        slot = tick + 1 - core

        for part in range(PARTS):
            def arrive(source, carry, part=part):
                wait_item(slot, part, source)
                return carry

            @pl.when(carrier(slot, part) != core)
            def _(arrive=arrive):
                lax.fori_loop(0, n_var, arrive, 0)

        for part, high, low in ((0, y_high, y_low), (1, d_high, d_low)):
            if shard % 16 == 0:
                def cut(source, carry, part=part, high=high, low=low):
                    rows = pl.ds(pl.multiple_of(source * shard, 16), shard)
                    high[rows, :], low[rows, :] = split(buf[slot, part, source])
                    return carry

                lax.fori_loop(0, n_var, cut, 0)
            else:
                for source in range(n_var):
                    stage[pl.ds(source * shard, shard), :] = buf[slot, part, source]
                high[...], low[...] = split(stage[...])

    def chunk(tick, c):
        rows = pl.ds(pl.multiple_of(c * height, height), height)
        rows_in = out_ref[rows, :]
        covar = dot3(rows_in, y_high[...], y_low[...], NT)
        taper_now = taper_ref[tick, rows, :].astype(jnp.float32)
        n_obs_blocks = mask_ref.shape[2]
        width = covar.shape[1] // n_obs_blocks
        strips = []
        for a in range(per_chunk):
            lines = slice(a * block, (a + 1) * block)
            pieces = []
            for b in range(n_obs_blocks):
                flag = mask_ref[tick, c * per_chunk + a, b].astype(jnp.float32)
                flag = flag * (1.0 / (members - 1))
                cols = slice(b * width, (b + 1) * width)
                pieces.append(taper_now[lines, cols] * covar[lines, cols] * flag)
            strips.append(jnp.concatenate(pieces, 1))
        weights = jnp.concatenate(strips, 0)
        out_ref[rows, :] = rows_in + dot3(weights, d_high[...], d_low[...], NN)

    def tick_now(tick):
        prepare(tick)

        def body(c, carry):
            chunk(tick, c)
            return carry

        lax.fori_loop(0, n_chunks, body, 0)

    far = n_z + n_x - 2
    last_step = N_UNITS - 1 + far
    early = jnp.logical_or(odd == 0, core == 1)
    for unit in range(AHEAD):
        gather_step(unit, 0)
    for step in range(last_step + 1):
        if step + AHEAD < N_UNITS:
            gather_step(step + AHEAD, 0)
        for unit in range(N_UNITS):
            if 1 <= step - unit <= far:
                gather_step(unit, step - unit)
        for unit in range(N_SHARED):
            if 0 <= step - unit - 1 <= far:
                shared_step(unit, step - unit - 1)
        if step == last_step - 1:
            state_load.wait()
            taper_load.wait()

            @pl.when(early)
            def _():
                tick_now(0)

    def later(tick, carry):
        tick_now(tick)
        return carry

    lax.fori_loop(early.astype(jnp.int32), ticks, later, 0)

    seeds(False)
    for unit in range(N_UNITS):
        slot, part, there = plane_unit(unit)

        def left(source, carry, unit=unit, slot=slot, part=part):
            copies(unit, slot, part, source // n_x, source % n_x, end)
            return carry

        @pl.when(there)
        def _(left=left):
            lax.fori_loop(0, n_var, left, 0)
    for unit in range(N_SHARED):
        slot, part, there = shared_unit(unit)

        def gone(source, carry, unit=unit, slot=slot, part=part):
            near_copy(slot, part, source, sent.at[N_UNITS + unit, source, 0], end)
            return carry

        @pl.when(there)
        def _(gone=gone):
            lax.fori_loop(0, n_var, gone, 0)


def on_device(n_region, n_var, state, taper, block_mask, anom_fly, incr_fly, anom_new, incr_new):
    ticks = taper.shape[0]
    shard, members = anom_fly.shape[1:]
    obs = shard * n_var
    n_x = 2 ** (int(math.log2(n_var)) // 2)
    slots = ticks + 1
    vmem = pl.BlockSpec(memory_space=pltpu.VMEM)
    anywhere = pl.BlockSpec(memory_space=pl.ANY)
    flops = 3 * 4 * ticks * state.shape[0] * obs * members
    return pl.pallas_call(
        functools.partial(kernel, n_region, n_var, n_x, ticks),
        out_shape=jax.ShapeDtypeStruct(state.shape, jnp.float32),
        in_specs=[pl.BlockSpec(memory_space=pltpu.SMEM)] + [anywhere] * 6,
        out_specs=vmem,
        scratch_shapes=[
            pltpu.VMEM((slots, PARTS, n_var, shard, members), jnp.float32),
            pltpu.VMEM(taper.shape, taper.dtype),
            pltpu.VMEM((obs, members), jnp.bfloat16),
            pltpu.VMEM((obs, members), jnp.bfloat16),
            pltpu.VMEM((obs, members), jnp.bfloat16),
            pltpu.VMEM((obs, members), jnp.bfloat16),
            pltpu.VMEM((8, 128) if shard % 16 == 0 else (obs, members), jnp.float32),
            pltpu.SemaphoreType.DMA((slots, PARTS, n_var)),
            pltpu.SemaphoreType.DMA((N_UNITS + N_SHARED, n_var, 6)),
            pltpu.SemaphoreType.DMA((3, CORES, PARTS)),
            pltpu.SemaphoreType.DMA((2,)),
        ],
        compiler_params=pltpu.CompilerParams(
            collective_id=0, has_side_effects=True, vmem_limit_bytes=60 * 1024 * 1024
        ),
        cost_estimate=pl.CostEstimate(
            flops=flops, bytes_accessed=4 * state.size * 4, transcendentals=0
        ),
        name="gather_and_assimilate",
    )(block_mask, state, taper, anom_fly, incr_fly, anom_new, incr_new)


def solution(mesh):
    n_region, n_var = mesh.shape["region"], mesh.shape["var"]
    in_specs = (
        P(("region", "var"), None),
        P(None, ("region", "var"), None),
        P(None, ("region", "var"), None),
        P("region", "var", None),
        P("region", "var", None),
        P(None, "var", None),
        P(None, "var", None),
    )
    out_specs = P(("region", "var"), None)
    return jax.shard_map(
        functools.partial(on_device, n_region, n_var),
        mesh=mesh, in_specs=in_specs, out_specs=out_specs, check_vma=False,
    )
```

time: 115 us -> 81 us (0.70)
  Pallas kernels: 106 us -> 76.1 us
  local copies, waits for them, and re-layouts: 8.6 us -> 4.04 us
    pallas_call x1, Pallas kernels: 106 us -> 76.1 us  [on_device(): pl.pallas_call(functools.partial(kernel, n_region, n_var, n_x, ticks), ou...]
    unnamed x14 -> x2, local copies, waits for them, and re-layouts: 8.6 us -> 4.04 us
where the time goes in v2:
time: 81 us; the launch traced here: 80.2 us
  Pallas kernels  76.1 us (94%)
  local copies, waits for them, and re-layouts  4.04 us (5%)
    pallas_call x1, Pallas kernels, on_device(): pl.pallas_call(functools.partial(kernel, n_region, n_var, n_x, ticks), ou...  76.1 us
    unnamed x2, local copies, waits for them, and re-layouts  4.04 us

profile of v2, /device:TPU:0, one launch (start us, length us, event | category | flops | bytes accessed | tf_op | source)
XLA Modules:
  0.0 80.2 jit_solution(16457803735739919508)
XLA Ops:
  0.0 1.4 %copy.8.mask_ref = s32[4,4,3]{2,1,0:T(4,128)} copy(s32[4,4,3]{1,0,2:T(4,128)} %param.9) | data formatting | bytes 384 | tf_op args[2]
  1.4 76.1 %gather_and_assimilate.1 = f32[512,768]{1,0:T(8,128)} custom-call(s32[4,4,3]{2,1,0:T(4,128)} %copy.8.mask_ref, f32[512,768]{1,0:T(8,128)} %state_ref.1, bf16[4,512,384]{2,1,0:T(8,128)(2,1)} %taper_hbm.1, f32[1,48,768]{2,1,0:T(8,128)} %anom_fly.1, f32[1,48,768]{2,1,0:T(8,128)} %incr_fly.1, f32[3,48,768]{2,1,0:T(8,128)} %anom_new.1, f32[3,48,768]{2,1,0:T(8,128)} %incr_new.1), custom_call_target="tpu_custom_call" | custom-call | flops 7247757312 | bytes 6291456 | tf_op jit(solution)/shard_map/gather_and_assimilate/pallas_call | solution.py:378
  77.5 2.7 %copy.10 = f32[512,768]{1,0:T(8,128)} copy(f32[512,768]{1,0:T(8,128)} %gather_and_assimilate.1) | data formatting | bytes 3145728

commit v3 on v2

--- a/solution.py
+++ b/solution.py
@@ -19,34 +19,29 @@
 }
 N_UNITS = 4
 N_SHARED = 3
-AHEAD = 2
+AHEAD = 4
 NT = (((1,), (1,)), ((), ()))
 NN = (((1,), (0,)), ((), ()))
+
+
+def dot(left, right, dims):
+    return lax.dot_general(left, right, dims, preferred_element_type=jnp.float32)
 
 
 def split(value):
     high = value.astype(jnp.bfloat16)
     return high, (value - high.astype(jnp.float32)).astype(jnp.bfloat16)
-
-
-def dot3(left, right_high, right_low, dims):
-    high, low = split(left)
-    rows = left.shape[0]
-    both = lax.dot_general(
-        jnp.concatenate([high, low], 0), right_high, dims, preferred_element_type=jnp.float32
-    )
-    cross = lax.dot_general(high, right_low, dims, preferred_element_type=jnp.float32)
-    return both[:rows] + (both[rows:] + cross)
 
 
 def kernel(
     n_region, n_var, n_x, ticks,
     mask_ref, state_ref, taper_hbm, anom_fly, incr_fly, anom_new, incr_new,
     out_ref,
-    buf, taper_ref, y_high, y_low, d_high, d_low, stage, recv, sent, seed_sent, load,
+    buf, taper_ref, halves, stage, recv, sent, seed_sent, load,
 ):
     slots = ticks + 1
     n_y, n_z = n_region // CORES, n_var // n_x
+    far = n_z + n_x - 2
     region, var = lax.axis_index("region"), lax.axis_index("var")
     y, core = region // CORES, region % CORES
     z, x = var // n_x, var % n_x
@@ -54,6 +49,8 @@
     fly, new = (anom_fly, incr_fly), (anom_new, incr_new)
     members = state_ref.shape[1]
     shard = buf.shape[3]
+    obs = shard * n_var
+    aligned = shard % 16 == 0
     block = state_ref.shape[0] // mask_ref.shape[1]
 
     state_load = pltpu.make_async_copy(state_ref, out_ref, load.at[0])
@@ -79,12 +76,6 @@
 
     def is_shared(parity, slot):
         return jnp.where(parity == 0, slot < N_SHARED, slot >= slots - N_SHARED)
-
-    def carrier(slot, part):
-        here = jnp.logical_and(is_shared(odd, slot), odd != part)
-        return jnp.where(
-            is_carried(odd, 0, slot, part), 0, jnp.where(here, part, 1)
-        )
 
     barrier = pltpu.get_barrier_semaphore()
     greeted = jnp.int32(0)
@@ -155,15 +146,27 @@
         here = buf.at[slot, part, source]
         pltpu.make_async_copy(here, here, recv.at[slot, part, source]).wait()
 
-    def plane_unit(unit):
+    def plane_unit(unit, mate):
         pairs = {key: units[min(unit, len(units) - 1)] for key, units in UNITS.items()}
-        slot = choose(odd, core, {key: pair[0] for key, pair in pairs.items()})
-        part = choose(odd, core, {key: pair[1] for key, pair in pairs.items()})
-        there = choose(odd, core, {key: unit < len(units) for key, units in UNITS.items()})
+        slot = choose(odd, mate, {key: pair[0] for key, pair in pairs.items()})
+        part = choose(odd, mate, {key: pair[1] for key, pair in pairs.items()})
+        there = choose(odd, mate, {key: unit < len(units) for key, units in UNITS.items()})
         return slot, part, there
 
-    def shared_unit(unit):
-        return unit + (slots - N_SHARED) * odd, 1 - odd, core != odd
+    def shared_unit(unit, mate):
+        return unit + (slots - N_SHARED) * odd, 1 - odd, mate != odd
+
+    def keep(slot, part, source):
+        if not aligned:
+            return
+        tick = slot - 1 + core
+
+        @pl.when(jnp.logical_and(tick >= 0, tick < ticks))
+        def _():
+            high, low = split(buf[slot, part, source])
+            start = pl.multiple_of(source * shard, 16)
+            halves[tick, part, pl.ds(start, shard), :] = high
+            halves[tick, part, pl.ds(start + obs, shard), :] = low
 
     def near_copy(slot, part, source, send_sem, act):
         @pl.when(jnp.where(core == 0, slot < slots - 1, slot > 0))
@@ -235,61 +238,69 @@
                 act(z_from, x_from)
 
     def gather_step(unit, hop):
-        slot, part, there = plane_unit(unit)
+        slot, part, there = plane_unit(unit, core)
 
         def handle(z_from, x_from):
             wait_item(slot, part, z_from * n_x + x_from)
             copies(unit, slot, part, z_from, x_from, begin)
+            keep(slot, part, z_from * n_x + x_from)
 
         @pl.when(there)
         def _():
             ring(hop, handle)
 
     def shared_step(unit, hop):
-        slot, part, there = shared_unit(unit)
+        slot, part, there = shared_unit(unit, core)
 
         def handle(z_from, x_from):
             source = z_from * n_x + x_from
             wait_item(slot, part, source)
             near_copy(slot, part, source, sent.at[N_UNITS + unit, source, 0], begin)
+            keep(slot, part, source)
 
         @pl.when(there)
         def _():
             ring(hop, handle)
 
+    def mate_step(step):
+        for count, lag, which in ((N_UNITS, 0, plane_unit), (N_SHARED, 1, shared_unit)):
+            for unit in range(count):
+                hop = step - unit - lag
+                if not 0 <= hop <= far:
+                    continue
+                slot, part, there = which(unit, 1 - core)
+                needed = jnp.logical_and(slot - 1 + core >= 0, slot - 1 + core < ticks)
+
+                def take(z_from, x_from, slot=slot, part=part):
+                    source = z_from * n_x + x_from
+                    wait_item(slot, part, source)
+                    keep(slot, part, source)
+
+                @pl.when(jnp.logical_and(there, needed))
+                def _(hop=hop, take=take):
+                    ring(hop, take)
+
     per_chunk = 2 if mask_ref.shape[1] % 2 == 0 else 1
     n_chunks = mask_ref.shape[1] // per_chunk
     height = per_chunk * block
 
     def prepare(tick):
+        if aligned:
+            return
         slot = tick + 1 - core
-
         for part in range(PARTS):
-            def arrive(source, carry, part=part):
-                wait_item(slot, part, source)
-                return carry
-
-            @pl.when(carrier(slot, part) != core)
-            def _(arrive=arrive):
-                lax.fori_loop(0, n_var, arrive, 0)
-
-        for part, high, low in ((0, y_high, y_low), (1, d_high, d_low)):
-            if shard % 16 == 0:
-                def cut(source, carry, part=part, high=high, low=low):
-                    rows = pl.ds(pl.multiple_of(source * shard, 16), shard)
-                    high[rows, :], low[rows, :] = split(buf[slot, part, source])
-                    return carry
-
-                lax.fori_loop(0, n_var, cut, 0)
-            else:
-                for source in range(n_var):
-                    stage[pl.ds(source * shard, shard), :] = buf[slot, part, source]
-                high[...], low[...] = split(stage[...])
+            for source in range(n_var):
+                stage[pl.ds(source * shard, shard), :] = buf[slot, part, source]
+            high, low = split(stage[...])
+            halves[tick, part, :obs, :] = high
+            halves[tick, part, obs:, :] = low
 
     def chunk(tick, c):
         rows = pl.ds(pl.multiple_of(c * height, height), height)
         rows_in = out_ref[rows, :]
-        covar = dot3(rows_in, y_high[...], y_low[...], NT)
+        high, low = split(rows_in)
+        pair = dot(high, halves[tick, 0], NT)
+        covar = pair[:, :obs] + (pair[:, obs:] + dot(low, halves[tick, 0, :obs, :], NT))
         taper_now = taper_ref[tick, rows, :].astype(jnp.float32)
         n_obs_blocks = mask_ref.shape[2]
         width = covar.shape[1] // n_obs_blocks
@@ -304,7 +315,9 @@
                 pieces.append(taper_now[lines, cols] * covar[lines, cols] * flag)
             strips.append(jnp.concatenate(pieces, 1))
         weights = jnp.concatenate(strips, 0)
-        out_ref[rows, :] = rows_in + dot3(weights, d_high[...], d_low[...], NN)
+        high, low = split(weights)
+        gain = dot(jnp.concatenate([high, high], 1), halves[tick, 1], NN)
+        out_ref[rows, :] = rows_in + (gain + dot(low, halves[tick, 1, :obs, :], NN))
 
     def tick_now(tick):
         prepare(tick)
@@ -315,7 +328,6 @@
 
         lax.fori_loop(0, n_chunks, body, 0)
 
-    far = n_z + n_x - 2
     last_step = N_UNITS - 1 + far
     early = jnp.logical_or(odd == 0, core == 1)
     for unit in range(AHEAD):
@@ -329,13 +341,18 @@
         for unit in range(N_SHARED):
             if 0 <= step - unit - 1 <= far:
                 shared_step(unit, step - unit - 1)
+        if 0 < step < last_step:
+            mate_step(step - 1)
         if step == last_step - 1:
+            mate_step(step)
             state_load.wait()
             taper_load.wait()
 
             @pl.when(early)
             def _():
                 tick_now(0)
+        elif step == last_step:
+            mate_step(step)
 
     def later(tick, carry):
         tick_now(tick)
@@ -345,7 +362,7 @@
 
     seeds(False)
     for unit in range(N_UNITS):
-        slot, part, there = plane_unit(unit)
+        slot, part, there = plane_unit(unit, core)
 
         def left(source, carry, unit=unit, slot=slot, part=part):
             copies(unit, slot, part, source // n_x, source % n_x, end)
@@ -355,7 +372,7 @@
         def _(left=left):
             lax.fori_loop(0, n_var, left, 0)
     for unit in range(N_SHARED):
-        slot, part, there = shared_unit(unit)
+        slot, part, there = shared_unit(unit, core)
 
         def gone(source, carry, unit=unit, slot=slot, part=part):
             near_copy(slot, part, source, sent.at[N_UNITS + unit, source, 0], end)
@@ -383,10 +400,7 @@
         scratch_shapes=[
             pltpu.VMEM((slots, PARTS, n_var, shard, members), jnp.float32),
             pltpu.VMEM(taper.shape, taper.dtype),
-            pltpu.VMEM((obs, members), jnp.bfloat16),
-            pltpu.VMEM((obs, members), jnp.bfloat16),
-            pltpu.VMEM((obs, members), jnp.bfloat16),
-            pltpu.VMEM((obs, members), jnp.bfloat16),
+            pltpu.VMEM((ticks, PARTS, 2 * obs, members), jnp.bfloat16),
             pltpu.VMEM((8, 128) if shard % 16 == 0 else (obs, members), jnp.float32),
             pltpu.SemaphoreType.DMA((slots, PARTS, n_var)),
             pltpu.SemaphoreType.DMA((N_UNITS + N_SHARED, n_var, 6)),

time: 81 us -> 78.1 us (0.964)
  Pallas kernels: 76.1 us -> 73 us
    pallas_call x1, Pallas kernels: 76.1 us -> 73 us  [on_device(): pl.pallas_call(functools.partial(kernel, n_region, n_var, n_x, ticks), ou...]
where the time goes in v3:
time: 78.1 us; the launch traced here: 77 us
  Pallas kernels  73 us (93%)
  local copies, waits for them, and re-layouts  4.04 us (5%)
    pallas_call x1, Pallas kernels, on_device(): pl.pallas_call(functools.partial(kernel, n_region, n_var, n_x, ticks), ou...  73 us
    unnamed x2, local copies, waits for them, and re-layouts  4.04 us

profile of v3, /device:TPU:0, one launch (start us, length us, event | category | flops | bytes accessed | tf_op | source)
XLA Modules:
  0.0 77.0 jit_solution(13070544668338627839)
XLA Ops:
  0.0 1.4 %copy.8.mask_ref = s32[4,4,3]{2,1,0:T(4,128)} copy(s32[4,4,3]{1,0,2:T(4,128)} %param.9) | data formatting | bytes 384 | tf_op args[2]
  1.4 73.0 %gather_and_assimilate.1 = f32[512,768]{1,0:T(8,128)} custom-call(s32[4,4,3]{2,1,0:T(4,128)} %copy.8.mask_ref, f32[512,768]{1,0:T(8,128)} %state_ref.1, bf16[4,512,384]{2,1,0:T(8,128)(2,1)} %taper_hbm.1, f32[1,48,768]{2,1,0:T(8,128)} %anom_fly.1, f32[1,48,768]{2,1,0:T(8,128)} %incr_fly.1, f32[3,48,768]{2,1,0:T(8,128)} %anom_new.1, f32[3,48,768]{2,1,0:T(8,128)} %incr_new.1), custom_call_target="tpu_custom_call" | custom-call | flops 7247757312 | bytes 6291456 | tf_op jit(solution)/shard_map/gather_and_assimilate/pallas_call | solution.py:395
  74.4 2.7 %copy.10 = f32[512,768]{1,0:T(8,128)} copy(f32[512,768]{1,0:T(8,128)} %gather_and_assimilate.1) | data formatting | bytes 3145728

commit v4 on v3

--- a/solution.py
+++ b/solution.py
@@ -19,7 +19,8 @@
 }
 N_UNITS = 4
 N_SHARED = 3
-AHEAD = 4
+AHEAD = 3
+LAG = 3
 NT = (((1,), (1,)), ((), ()))
 NN = (((1,), (0,)), ((), ()))
 
@@ -35,9 +36,9 @@
 
 def kernel(
     n_region, n_var, n_x, ticks,
-    mask_ref, state_ref, taper_hbm, anom_fly, incr_fly, anom_new, incr_new,
+    mask_hbm, state_ref, taper_hbm, anom_fly, incr_fly, anom_new, incr_new,
     out_ref,
-    buf, taper_ref, halves, stage, recv, sent, seed_sent, load,
+    buf, taper_ref, mask_ref, halves, stage, recv, sent, seed_sent, load,
 ):
     slots = ticks + 1
     n_y, n_z = n_region // CORES, n_var // n_x
@@ -55,6 +56,8 @@
 
     state_load = pltpu.make_async_copy(state_ref, out_ref, load.at[0])
     taper_load = pltpu.make_async_copy(taper_hbm, taper_ref, load.at[1])
+    mask_load = pltpu.make_async_copy(mask_hbm, mask_ref, load.at[2])
+    mask_load.start()
     state_load.start()
     taper_load.start()
 
@@ -243,7 +246,6 @@
         def handle(z_from, x_from):
             wait_item(slot, part, z_from * n_x + x_from)
             copies(unit, slot, part, z_from, x_from, begin)
-            keep(slot, part, z_from * n_x + x_from)
 
         @pl.when(there)
         def _():
@@ -256,24 +258,24 @@
             source = z_from * n_x + x_from
             wait_item(slot, part, source)
             near_copy(slot, part, source, sent.at[N_UNITS + unit, source, 0], begin)
-            keep(slot, part, source)
 
         @pl.when(there)
         def _():
             ring(hop, handle)
 
-    def mate_step(step):
+    def take_step(step, mate):
         for count, lag, which in ((N_UNITS, 0, plane_unit), (N_SHARED, 1, shared_unit)):
             for unit in range(count):
                 hop = step - unit - lag
                 if not 0 <= hop <= far:
                     continue
-                slot, part, there = which(unit, 1 - core)
+                slot, part, there = which(unit, mate)
                 needed = jnp.logical_and(slot - 1 + core >= 0, slot - 1 + core < ticks)
 
                 def take(z_from, x_from, slot=slot, part=part):
                     source = z_from * n_x + x_from
-                    wait_item(slot, part, source)
+                    if mate is not core:
+                        wait_item(slot, part, source)
                     keep(slot, part, source)
 
                 @pl.when(jnp.logical_and(there, needed))
@@ -329,6 +331,7 @@
         lax.fori_loop(0, n_chunks, body, 0)
 
     last_step = N_UNITS - 1 + far
+    other = 1 - core
     early = jnp.logical_or(odd == 0, core == 1)
     for unit in range(AHEAD):
         gather_step(unit, 0)
@@ -342,17 +345,23 @@
             if 0 <= step - unit - 1 <= far:
                 shared_step(unit, step - unit - 1)
         if 0 < step < last_step:
-            mate_step(step - 1)
+            take_step(step - 1, core)
+        if LAG <= step < last_step - 1:
+            take_step(step - LAG, other)
         if step == last_step - 1:
-            mate_step(step)
+            take_step(step, core)
+            for taken in range(step - LAG, last_step):
+                take_step(taken, other)
             state_load.wait()
             taper_load.wait()
+            mask_load.wait()
 
             @pl.when(early)
             def _():
                 tick_now(0)
         elif step == last_step:
-            mate_step(step)
+            take_step(step, core)
+            take_step(step, other)
 
     def later(tick, carry):
         tick_now(tick)
@@ -395,17 +404,18 @@
     return pl.pallas_call(
         functools.partial(kernel, n_region, n_var, n_x, ticks),
         out_shape=jax.ShapeDtypeStruct(state.shape, jnp.float32),
-        in_specs=[pl.BlockSpec(memory_space=pltpu.SMEM)] + [anywhere] * 6,
+        in_specs=[anywhere] * 7,
         out_specs=vmem,
         scratch_shapes=[
             pltpu.VMEM((slots, PARTS, n_var, shard, members), jnp.float32),
             pltpu.VMEM(taper.shape, taper.dtype),
+            pltpu.SMEM(block_mask.shape, block_mask.dtype),
             pltpu.VMEM((ticks, PARTS, 2 * obs, members), jnp.bfloat16),
             pltpu.VMEM((8, 128) if shard % 16 == 0 else (obs, members), jnp.float32),
             pltpu.SemaphoreType.DMA((slots, PARTS, n_var)),
             pltpu.SemaphoreType.DMA((N_UNITS + N_SHARED, n_var, 6)),
             pltpu.SemaphoreType.DMA((3, CORES, PARTS)),
-            pltpu.SemaphoreType.DMA((2,)),
+            pltpu.SemaphoreType.DMA((3,)),
         ],
         compiler_params=pltpu.CompilerParams(
             collective_id=0, has_side_effects=True, vmem_limit_bytes=60 * 1024 * 1024

time: 78.1 us -> 77.9 us (level); the launches traced: 77 us -> 77.7 us
  no operation moved by 1% of the time
where the time goes in v4:
time: 77.9 us; the launch traced here: 77.7 us
  Pallas kernels  73.7 us (95%)
  local copies, waits for them, and re-layouts  4.04 us (5%)
    pallas_call x1, Pallas kernels, on_device(): pl.pallas_call(functools.partial(kernel, n_region, n_var, n_x, ticks), ou...  73.7 us
    unnamed x2, local copies, waits for them, and re-layouts  4.04 us

profile of v4, /device:TPU:0, one launch (start us, length us, event | category | flops | bytes accessed | tf_op | source)
XLA Modules:
  0.0 77.7 jit_solution(1815241199189788133)
XLA Ops:
  0.0 1.4 %copy.8.mask_hbm = s32[4,4,3]{2,1,0:T(4,128)} copy(s32[4,4,3]{1,0,2:T(4,128)} %param.9) | data formatting | bytes 384 | tf_op args[2]
  1.4 73.7 %gather_and_assimilate.1 = f32[512,768]{1,0:T(8,128)} custom-call(s32[4,4,3]{2,1,0:T(4,128)} %copy.8.mask_hbm, f32[512,768]{1,0:T(8,128)} %state_ref.1, bf16[4,512,384]{2,1,0:T(8,128)(2,1)} %taper_hbm.1, f32[1,48,768]{2,1,0:T(8,128)} %anom_fly.1, f32[1,48,768]{2,1,0:T(8,128)} %incr_fly.1, f32[3,48,768]{2,1,0:T(8,128)} %anom_new.1, f32[3,48,768]{2,1,0:T(8,128)} %incr_new.1), custom_call_target="tpu_custom_call" | custom-call | flops 7247757312 | bytes 6291456 | tf_op jit(solution)/shard_map/gather_and_assimilate/pallas_call | solution.py:404
  75.1 2.7 %copy.10 = f32[512,768]{1,0:T(8,128)} copy(f32[512,768]{1,0:T(8,128)} %gather_and_assimilate.1) | data formatting | bytes 3145728

commit v5 on v4

--- a/solution.py
+++ b/solution.py
@@ -14,8 +14,8 @@
 UNITS = {
     (0, 0): ((0, 0), (1, 0), (2, 0), (3, 0)),
     (0, 1): ((3, 1), (4, 1), (4, 0)),
-    (1, 0): ((0, 0), (0, 1), (1, 0), (1, 1)),
-    (1, 1): ((2, 1), (3, 1), (4, 1)),
+    (1, 0): ((0, 0), (0, 1), (1, 0)),
+    (1, 1): ((2, 1), (1, 1), (3, 1), (4, 1)),
 }
 N_UNITS = 4
 N_SHARED = 3
@@ -38,7 +38,7 @@
     n_region, n_var, n_x, ticks,
     mask_hbm, state_ref, taper_hbm, anom_fly, incr_fly, anom_new, incr_new,
     out_ref,
-    buf, taper_ref, mask_ref, halves, stage, recv, sent, seed_sent, load,
+    buf, taper_ref, mask_ref, ready, halves, stage, recv, sent, seed_sent, load,
 ):
     slots = ticks + 1
     n_y, n_z = n_region // CORES, n_var // n_x
@@ -52,7 +52,7 @@
     shard = buf.shape[3]
     obs = shard * n_var
     aligned = shard % 16 == 0
-    block = state_ref.shape[0] // mask_ref.shape[1]
+    block = state_ref.shape[0] // mask_ref.shape[2]
 
     state_load = pltpu.make_async_copy(state_ref, out_ref, load.at[0])
     taper_load = pltpu.make_async_copy(taper_hbm, taper_ref, load.at[1])
@@ -282,57 +282,60 @@
                 def _(hop=hop, take=take):
                     ring(hop, take)
 
-    per_chunk = 2 if mask_ref.shape[1] % 2 == 0 else 1
-    n_chunks = mask_ref.shape[1] // per_chunk
+    per_chunk = 2 if mask_ref.shape[2] % 2 == 0 else 1
+    n_chunks = mask_ref.shape[2] // per_chunk
     height = per_chunk * block
 
-    def prepare(tick):
+    def prepare(tick, parts=range(PARTS)):
         if aligned:
             return
         slot = tick + 1 - core
-        for part in range(PARTS):
+        for part in parts:
             for source in range(n_var):
                 stage[pl.ds(source * shard, shard), :] = buf[slot, part, source]
             high, low = split(stage[...])
             halves[tick, part, :obs, :] = high
             halves[tick, part, obs:, :] = low
 
-    def chunk(tick, c):
+    def weigh(tick, c):
         rows = pl.ds(pl.multiple_of(c * height, height), height)
         rows_in = out_ref[rows, :]
         high, low = split(rows_in)
         pair = dot(high, halves[tick, 0], NT)
         covar = pair[:, :obs] + (pair[:, obs:] + dot(low, halves[tick, 0, :obs, :], NT))
         taper_now = taper_ref[tick, rows, :].astype(jnp.float32)
-        n_obs_blocks = mask_ref.shape[2]
+        n_obs_blocks = mask_ref.shape[0]
         width = covar.shape[1] // n_obs_blocks
         strips = []
         for a in range(per_chunk):
             lines = slice(a * block, (a + 1) * block)
             pieces = []
             for b in range(n_obs_blocks):
-                flag = mask_ref[tick, c * per_chunk + a, b].astype(jnp.float32)
+                flag = mask_ref[b, tick, c * per_chunk + a].astype(jnp.float32)
                 flag = flag * (1.0 / (members - 1))
                 cols = slice(b * width, (b + 1) * width)
                 pieces.append(taper_now[lines, cols] * covar[lines, cols] * flag)
             strips.append(jnp.concatenate(pieces, 1))
         weights = jnp.concatenate(strips, 0)
-        high, low = split(weights)
+        return split(weights)
+
+    def apply(tick, c, high, low):
+        rows = pl.ds(pl.multiple_of(c * height, height), height)
         gain = dot(jnp.concatenate([high, high], 1), halves[tick, 1], NN)
-        out_ref[rows, :] = rows_in + (gain + dot(low, halves[tick, 1, :obs, :], NN))
+        gain = gain + dot(low, halves[tick, 1, :obs, :], NN)
+        out_ref[rows, :] = out_ref[rows, :] + gain
 
     def tick_now(tick):
         prepare(tick)
 
         def body(c, carry):
-            chunk(tick, c)
+            apply(tick, c, *weigh(tick, c))
             return carry
 
         lax.fori_loop(0, n_chunks, body, 0)
 
     last_step = N_UNITS - 1 + far
     other = 1 - core
-    early = jnp.logical_or(odd == 0, core == 1)
     for unit in range(AHEAD):
         gather_step(unit, 0)
     for step in range(last_step + 1):
@@ -356,9 +359,15 @@
             taper_load.wait()
             mask_load.wait()
 
-            @pl.when(early)
-            def _():
-                tick_now(0)
+            tick_now(0)
+            prepare(1, (0,))
+
+            def weigh_next(c, carry):
+                rows = pl.ds(pl.multiple_of(c * height, height), height)
+                ready[0, rows, :], ready[1, rows, :] = weigh(1, c)
+                return carry
+
+            lax.fori_loop(0, n_chunks, weigh_next, 0)
         elif step == last_step:
             take_step(step, core)
             take_step(step, other)
@@ -367,7 +376,14 @@
         tick_now(tick)
         return carry
 
-    lax.fori_loop(early.astype(jnp.int32), ticks, later, 0)
+    def apply_ready(c, carry):
+        rows = pl.ds(pl.multiple_of(c * height, height), height)
+        apply(1, c, ready[0, rows, :], ready[1, rows, :])
+        return carry
+
+    prepare(1, (1,))
+    lax.fori_loop(0, n_chunks, apply_ready, 0)
+    lax.fori_loop(2, ticks, later, 0)
 
     seeds(False)
     for unit in range(N_UNITS):
@@ -398,6 +414,7 @@
     obs = shard * n_var
     n_x = 2 ** (int(math.log2(n_var)) // 2)
     slots = ticks + 1
+    block_mask = jnp.transpose(block_mask, (2, 0, 1))
     vmem = pl.BlockSpec(memory_space=pltpu.VMEM)
     anywhere = pl.BlockSpec(memory_space=pl.ANY)
     flops = 3 * 4 * ticks * state.shape[0] * obs * members
@@ -410,6 +427,7 @@
             pltpu.VMEM((slots, PARTS, n_var, shard, members), jnp.float32),
             pltpu.VMEM(taper.shape, taper.dtype),
             pltpu.SMEM(block_mask.shape, block_mask.dtype),
+            pltpu.VMEM((2, state.shape[0], obs), jnp.bfloat16),
             pltpu.VMEM((ticks, PARTS, 2 * obs, members), jnp.bfloat16),
             pltpu.VMEM((8, 128) if shard % 16 == 0 else (obs, members), jnp.float32),
             pltpu.SemaphoreType.DMA((slots, PARTS, n_var)),

time: 77.9 us -> 85.4 us (1.096)
  Pallas kernels: 73.7 us -> 82.6 us
  local copies, waits for them, and re-layouts: 4.04 us -> 2.65 us
    pallas_call x1, Pallas kernels: 73.7 us -> 82.6 us  [on_device(): pl.pallas_call(functools.partial(kernel, n_region, n_var, n_x, ticks), ou...]
    unnamed x2 -> x1, local copies, waits for them, and re-layouts: 4.04 us -> 2.65 us
where the time goes in v5:
time: 85.4 us; the launch traced here: 85.3 us
  Pallas kernels  82.6 us (97%)
  local copies, waits for them, and re-layouts  2.65 us (3%)
    pallas_call x1, Pallas kernels, on_device(): pl.pallas_call(functools.partial(kernel, n_region, n_var, n_x, ticks), ou...  82.6 us
    unnamed x1, local copies, waits for them, and re-layouts  2.65 us

profile of v5, /device:TPU:0, one launch (start us, length us, event | category | flops | bytes accessed | tf_op | source)
XLA Modules:
  0.0 85.3 jit_solution(10687217274194214840)
XLA Ops:
  0.0 82.6 %gather_and_assimilate.1 = f32[512,768]{1,0:T(8,128)} custom-call(s32[3,4,4]{2,1,0:T(4,128)} %bitcast.1, f32[512,768]{1,0:T(8,128)} %state_ref.1, bf16[4,512,384]{2,1,0:T(8,128)(2,1)} %taper_hbm.1, f32[1,48,768]{2,1,0:T(8,128)} %anom_fly.1, f32[1,48,768]{2,1,0:T(8,128)} %incr_fly.1, f32[3,48,768]{2,1,0:T(8,128)} %anom_new.1, f32[3,48,768]{2,1,0:T(8,128)} %incr_new.1), custom_call_target="tpu_custom_call" | custom-call | flops 7247757312 | bytes 6291456 | tf_op jit(solution)/shard_map/gather_and_assimilate/pallas_call | solution.py:421
  82.6 2.7 %copy.9 = f32[512,768]{1,0:T(8,128)} copy(f32[512,768]{1,0:T(8,128)} %gather_and_assimilate.1) | data formatting | bytes 3145728
